TPU v7x, 256 devices: a whole 4x4x8 slice. The times are simulated.
256 devices in a mesh: vocab: 32 (over y, x, core), dp: 8 (over z).
Axes of the slice: x: 4, y: 4, z: 8, core: 2. Of those that a mesh axis runs over, the one named last changes fastest.
Arguments:
- hidden: bfloat16 [1024, 4096], P('vocab', 'dp'), may hold values from -6 to 6
- head_weight: bfloat16 [4096, 65536], P('dp', 'vocab'), may hold values from -0.09375 to 0.09375
- grad_pooled: float32 [16, 65536], P(None, 'vocab'), may hold values from -6 to 6
- lengths: int32 [16], replicated, may hold values from 32 to 96, as said below
- argmax_local: int32 [16, 65536], P(None, 'vocab'), may hold values from 0 to 95, as said below
Outputs:
- grad_hidden: bfloat16 [1024, 4096], P('vocab', 'dp')
- grad_weight: bfloat16 [4096, 65536], P('dp', 'vocab')
Inputs may be any that keep to these rules, and one draw needn't show every extreme that they name: The lengths sum to 1024. argmax_local[p, v] is less than lengths[p].
All inputs are finite; a program needn't handle non-finite values.
Results may differ from a plain program's by a relative error of at most 0.02.
Values may be sent and summed in bfloat16 or wider, within the bound.
A program may use at most 64 MiB of HBM per device.

v0:
```python
import functools

import jax
import jax.numpy as jnp
from jax import lax
from jax.experimental import pallas as pl
from jax.experimental.pallas import tpu as pltpu
from jax.sharding import PartitionSpec as P

flops_weight = 3.0
MESH = pl.DeviceIdType.MESH
f32, bf16 = jnp.float32, jnp.bfloat16
CUT = 4
PIECES = 2


def kernel(
    ny, nx, nz,
    len_hbm, hid, w_hbm, gp_hbm, am_hbm,
    gh, gw,
    rows, rows_t, w, w_t, mask, dl, am, gp, e, e_t, part, give, take, slopes,
    twin_out, twin_in, rsend, rrecv, len_ref,
    loc_sem, ag_s, ag_r, tw_s, tw_r, x1_s, x1_r, x2_s, x2_r, gt_s, gt_r, rs_s, rs_r,
):
    chips = ny * nx
    me, z = lax.axis_index("vocab"), lax.axis_index("dp")
    core, chip = lax.rem(me, 2), lax.div(me, 2)
    x, y = lax.rem(chip, nx), lax.div(chip, nx)
    mate = 1 - core
    twin = chip * 2 + mate
    tb, feats = hid.shape
    terms = w.shape[1]
    passages = len_hbm.shape[0]
    band = nx * tb
    share = terms // nz
    wide = terms // CUT

    def to(src, dst, s, r, device):
        return pltpu.make_async_remote_copy(
            src_ref=src, dst_ref=dst, send_sem=s, recv_sem=r, device_id=device, device_id_type=MESH
        )

    near = lambda n: sorted(range(n), key=lambda d: (min(d, n - d), d))
    offsets = [(dy, dx) for dy in near(ny) for dx in near(nx)]
    far_xy = sorted(offsets[1:], key=lambda o: -min(o[0], ny - o[0]) - min(o[1], nx - o[1]))
    far_z = near(nz)[:0:-1]
    other = lambda dy, dx: (lax.rem(y + dy, ny), lax.rem(x + dx, nx))

    barrier = pltpu.get_barrier_semaphore()
    for dy, dx in far_xy:
        oy, ox = other(dy, dx)
        pl.semaphore_signal(barrier, inc=1, device_id={"vocab": (oy * nx + ox) * 2 + core}, device_id_type=MESH)
    pl.semaphore_signal(barrier, inc=1, device_id={"vocab": twin}, device_id_type=MESH)
    for k in far_z:
        pl.semaphore_signal(barrier, inc=1, device_id={"dp": lax.rem(z + k, nz)}, device_id_type=MESH)

    local = [
        pltpu.make_async_copy(hid, rows.at[core, y, x], loc_sem.at[0]),
        pltpu.make_async_copy(len_hbm, len_ref, loc_sem.at[4]),
        pltpu.make_async_copy(am_hbm, am, loc_sem.at[1]),
        pltpu.make_async_copy(w_hbm, w, loc_sem.at[2]),
        pltpu.make_async_copy(gp_hbm.at[:, pl.ds(pl.multiple_of(z * share, share), share)], gp, loc_sem.at[3]),
    ]
    for copy in local:
        copy.start()

    local[0].wait()
    pl.semaphore_wait(barrier, chips + nz - 1)

    gather = []
    for dy, dx in far_xy:
        oy, ox = other(dy, dx)
        at = oy * nx + ox
        copy = to(rows.at[core, y, x], rows.at[core, y, x], ag_s.at[at], ag_r.at[chip], {"vocab": at * 2 + core})
        copy.start()
        gather.append(copy)

    local[1].wait()
    starts, begin = [], jnp.int32(0)
    for p in range(passages):
        starts.append(begin)
        begin = begin + len_ref[p]
    ends = starts[1:] + [begin]

    def tokens(shape, dim, c, g):
        i = lax.broadcasted_iota(jnp.int32, shape, dim)
        return i + jnp.bitwise_and(i, -tb) + (g * 2 * band + c * tb)

    lane = lax.broadcasted_iota(jnp.int32, (band, passages), 1)
    first = jnp.zeros((band, passages), jnp.int32)
    last = jnp.zeros((band, passages), jnp.int32)
    sub = lax.broadcasted_iota(jnp.int32, (passages, band), 0)
    first_t = jnp.zeros((passages, band), jnp.int32)
    last_t = jnp.zeros((passages, band), jnp.int32)
    for p in range(passages):
        first = jnp.where(lane == p, starts[p], first)
        last = jnp.where(lane == p, ends[p], last)
        first_t = jnp.where(sub == p, starts[p], first_t)
        last_t = jnp.where(sub == p, ends[p], last_t)
    for c in range(2):
        for g in range(ny):
            token = tokens((band, passages), 0, c, g)
            e[c, g] = jnp.where((token >= first) & (token < last), 1.0, 0.0).astype(bf16)
            token = tokens((passages, band), 1, c, g)
            e_t[c, g] = jnp.where((token >= first_t) & (token < last_t), 1.0, 0.0).astype(bf16)
    local[2].wait()

    def mark(c, carry):
        places = []
        for g in range(ny):
            token = tokens((band, 1), 0, c, g)
            place = token
            for p in range(1, passages):
                place = jnp.where(token >= starts[p], token - starts[p], place)
            places.append(place)
        place = jnp.concatenate(places, axis=0).astype(f32)
        member = e[c].reshape(ny * band, passages)
        for n in range(CUT):
            cols = slice(n * wide, (n + 1) * wide)
            spread = jnp.dot(member, am[:, cols].astype(f32).astype(bf16), preferred_element_type=f32)
            mask[c, :, :, cols] = jnp.where(spread == place, 1.0, 0.0).astype(bf16).reshape(ny, band, wide)
        return carry

    lax.fori_loop(0, 2, mark, 0)
    local[3].wait()
    for n in range(CUT):
        w_t[n * wide:(n + 1) * wide, :] = w[:, n * wide:(n + 1) * wide].T

    def pick(c, bands, start):
        block = jnp.concatenate([rows[c, g].reshape(band, feats) for g in bands], axis=0)
        member = jnp.concatenate([e_t[c, g] for g in bands], axis=1)
        logits = jnp.dot(block, w[...], preferred_element_type=f32)
        marks = jnp.concatenate([mask[c, g] for g in bands], axis=0)
        found = jnp.dot(member, logits.astype(bf16) * marks, preferred_element_type=f32)
        for j in range(nz):
            piece = found[:, j * share:(j + 1) * share]
            part[j] = piece if start else part[j] + piece

    near_y = near(ny)
    pairs = [near_y[::-1][:ny // 2], near_y[::-1][ny // 2:]]
    far_y = near_y[::-1]
    parts = [far_y[::2], far_y[1::2]]
    forward = []

    def bands_of(pair):
        return [lax.rem(y + dy, ny) for dy in pair]

    def arrive(pair):
        for dy, g in zip(pair, bands_of(pair)):
            for dx in near(nx):
                if dy or dx:
                    oy, ox = other(dy, dx)
                    at = oy * nx + ox
                    to(rows.at[core, oy, ox], rows.at[core, oy, ox], ag_s.at[at], ag_r.at[at], {"vocab": twin}).wait_recv()
            copy = to(rows.at[core, g], rows.at[core, g], tw_s.at[dy], tw_r.at[dy], {"vocab": twin})
            copy.start()
            forward.append(copy)

    def lent(pair):
        for dy, g in zip(pair, bands_of(pair)):
            to(rows.at[mate, g], rows.at[mate, g], tw_s.at[dy], tw_r.at[dy], {"vocab": twin}).wait_recv()

    first_pair, second_pair = pairs
    arrive(first_pair)
    pick(core, bands_of(first_pair), True)
    arrive(second_pair)
    lent(first_pair)
    pick(mate, bands_of(first_pair), False)
    pick(core, bands_of(second_pair), False)
    lent(second_pair)
    pick(mate, bands_of(second_pair), False)

    for j in range(nz):
        give[j] = part[j].astype(bf16)
    ask = []
    for k in far_z:
        oz = lax.rem(z + k, nz)
        copy = to(give.at[oz], take.at[z], x1_s.at[oz], x1_r.at[z], {"dp": oz})
        copy.start()
        ask.append(copy)
    take[z] = give[z]
    for k in far_z:
        oz = lax.rem(z + k, nz)
        to(give.at[oz], take.at[oz], x1_s.at[oz], x1_r.at[oz], {"dp": oz}).wait_recv()
    local[4].wait()
    picked = take[0].astype(f32)
    for j in range(1, nz):
        picked = picked + take[j].astype(f32)
    small = jnp.exp(-jnp.abs(picked))
    soft = jnp.maximum(picked, 0.0) + jnp.log1p(small)
    column = jnp.sum(jnp.log1p(soft), axis=0, keepdims=True)
    upstream = gp[...] + 2.0 * flops_weight / (passages * passages) * column
    sigmoid = jnp.where(picked >= 0, 1.0, small) / (1.0 + small)
    slopes[z] = (upstream * sigmoid / (1.0 + soft)).astype(bf16)
    answer = []
    for k in far_z:
        oz = lax.rem(z + k, nz)
        copy = to(slopes.at[z], slopes.at[z], x2_s.at[oz], x2_r.at[z], {"dp": oz})
        copy.start()
        answer.append(copy)
    for k in far_z:
        oz = lax.rem(z + k, nz)
        to(slopes.at[z], slopes.at[oz], x2_s.at[oz], x2_r.at[oz], {"dp": oz}).wait_recv()

    def spread_slopes(c, bands):
        member = jnp.concatenate([e[c, g] for g in bands], axis=0)
        slope = jnp.concatenate([slopes[j] for j in range(nz)], axis=1)
        wider = jnp.dot(member, slope, preferred_element_type=f32).astype(bf16)
        for i, g in enumerate(bands):
            dl[c, g] = wider[i * band:(i + 1) * band] * mask[c, g]

    def hidden_part(c, bands):
        block = jnp.concatenate([dl[c, g] for g in bands], axis=0)
        return jnp.dot(block, w_t[...], preferred_element_type=f32)

    scatter, halves = [], []
    for pair in parts:
        bands = [lax.rem(y + dy, ny) for dy in pair]
        spread_slopes(mate, bands)
        total = hidden_part(mate, bands).astype(bf16)
        for i, dy in enumerate(pair):
            twin_out[dy] = total[i * band:(i + 1) * band]
            copy = to(twin_out.at[dy], twin_in.at[dy], gt_s.at[dy], gt_r.at[dy], {"vocab": twin})
            copy.start()
            halves.append(copy)
    for pair in parts:
        bands = [lax.rem(y + dy, ny) for dy in pair]
        spread_slopes(core, bands)
        total = hidden_part(core, bands)
        for i, (dy, g) in enumerate(zip(pair, bands)):
            to(twin_out.at[dy], twin_in.at[dy], gt_s.at[dy], gt_r.at[dy], {"vocab": twin}).wait_recv()
            both = total[i * band:(i + 1) * band] + twin_in[dy].astype(f32)
            rsend[g] = both.astype(bf16).reshape(nx, tb, feats)
            for dx in near(nx)[::-1]:
                if dy or dx:
                    oy, ox = other(dy, dx)
                    at = oy * nx + ox
                    copy = to(rsend.at[oy, ox], rrecv.at[chip], rs_s.at[at], rs_r.at[chip], {"vocab": at * 2 + core})
                    copy.start()
                    scatter.append(copy)

    for c in range(2):
        rows_t[:, c * ny * band:(c + 1) * ny * band] = rows[c].reshape(ny * band, feats).T
    block = dl[...].reshape(2 * ny * band, terms)
    gw[...] = jnp.dot(rows_t[...], block, preferred_element_type=f32).astype(bf16)

    rrecv[chip] = rsend[y, x]
    for copy in gather + forward + ask + answer + halves:
        copy.wait_send()
    for dy, dx in offsets[1:]:
        oy, ox = other(dy, dx)
        at = oy * nx + ox
        to(rsend.at[oy, ox], rrecv.at[at], rs_s.at[at], rs_r.at[at], {"vocab": twin}).wait_recv()
    total = rrecv[0].astype(f32)
    for k in range(1, chips):
        total = total + rrecv[k].astype(f32)
    gh[...] = total.astype(bf16)
    for copy in scatter:
        copy.wait_send()


def finish(gh, gw, gh_out, gw_out, sem):
    high = gw.shape[0] // PIECES
    copies = [
        pltpu.make_async_copy(gw.at[pl.ds(n * high, high)], gw_out.at[pl.ds(n * high, high)], sem.at[n])
        for n in range(PIECES)
    ]
    copies.append(pltpu.make_async_copy(gh, gh_out, sem.at[PIECES]))
    for copy in copies:
        copy.start()
    for copy in copies:
        copy.wait()


def per_device(nx, nz, hidden, head_weight, grad_pooled, lengths, argmax_local):
    tb, feats = hidden.shape
    terms = head_weight.shape[1]
    passages = lengths.shape[0]
    chips = lax.axis_size("vocab") // 2
    ny = chips // nx
    band = nx * tb
    tokens = 2 * ny * band
    share = terms // nz
    anywhere = pl.BlockSpec(memory_space=pl.ANY)
    dma = pltpu.SemaphoreType.DMA
    gh, gw = pl.pallas_call(
        functools.partial(kernel, ny, nx, nz),
        out_shape=(pltpu.VMEM((tb, feats), bf16), pltpu.VMEM((feats, terms), bf16)),
        in_specs=[anywhere] * 5,
        out_specs=(pl.BlockSpec(memory_space=pltpu.VMEM), pl.BlockSpec(memory_space=pltpu.VMEM)),
        scratch_shapes=[
            pltpu.VMEM((2, ny, nx, tb, feats), bf16),
            pltpu.VMEM((feats, tokens), bf16),
            pltpu.VMEM((feats, terms), bf16),
            pltpu.VMEM((terms, feats), bf16),
            pltpu.VMEM((2, ny, band, terms), bf16),
            pltpu.VMEM((2, ny, band, terms), bf16),
            pltpu.VMEM((passages, terms), jnp.int32),
            pltpu.VMEM((passages, share), f32),
            pltpu.VMEM((2, ny, band, passages), bf16),
            pltpu.VMEM((2, ny, passages, band), bf16),
            pltpu.VMEM((nz, passages, share), f32),
            pltpu.VMEM((nz, passages, share), bf16),
            pltpu.VMEM((nz, passages, share), bf16),
            pltpu.VMEM((nz, passages, share), bf16),
            pltpu.VMEM((ny, band, feats), bf16),
            pltpu.VMEM((ny, band, feats), bf16),
            pltpu.VMEM((ny, nx, tb, feats), bf16),
            pltpu.VMEM((chips, tb, feats), bf16),
            pltpu.SMEM((passages,), jnp.int32),
            dma((5,)),
            dma((chips,)), dma((chips,)),
            dma((ny,)), dma((ny,)),
            dma((nz,)), dma((nz,)),
            dma((nz,)), dma((nz,)),
            dma((ny,)), dma((ny,)),
            dma((chips,)), dma((chips,)),
        ],
        compiler_params=pltpu.CompilerParams(
            collective_id=0, has_side_effects=True, vmem_limit_bytes=56 * 1024 * 1024
        ),
        cost_estimate=pl.CostEstimate(
            flops=6 * tokens * feats * terms, bytes_accessed=4 * feats * terms, transcendentals=0
        ),
    )(lengths, hidden, head_weight, grad_pooled, argmax_local)
    return pl.pallas_call(
        finish,
        out_shape=(
            jax.ShapeDtypeStruct((tb, feats), bf16),
            jax.ShapeDtypeStruct((feats, terms), bf16),
        ),
        in_specs=[anywhere] * 2,
        out_specs=(anywhere, anywhere),
        scratch_shapes=[dma((PIECES + 1,))],
        compiler_params=pltpu.CompilerParams(vmem_limit_bytes=1024 * 1024),
    )(gh, gw)


def solution(mesh):
    in_specs = (P("vocab", "dp"), P("dp", "vocab"), P(None, "vocab"), P(), P(None, "vocab"))
    out_specs = (P("vocab", "dp"), P("dp", "vocab"))
    nx = 4 if mesh.shape["vocab"] == 32 else 2
    return jax.shard_map(
        functools.partial(per_device, nx, mesh.shape["dp"]),
        mesh=mesh, in_specs=in_specs, out_specs=out_specs, check_vma=False,
    )
```

profile of v0, /device:TPU:1, one launch (start us, length us, event | category | flops | bytes accessed | tf_op | source)
XLA Modules:
  0.0 43.8 jit_solution(11385738624608056307)
XLA Ops:
  0.6 41.8 %shard_map.68 = (bf16[32,512]{1,0:T(8,128)(2,1)S(1)}, bf16[512,2048]{1,0:T(8,128)(2,1)S(1)}) custom-call(s32[16]{0:T(128)} %len_hbm.1, bf16[32,512]{1,0:T(8,128)(2,1)} %hid.1, bf16[512,2048]{1,0:T(8,128)(2,1)} %w_hbm.1, f32[16,2048]{1,0:T(8,128)} %gp_hbm.1, s32[16,2048]{1,0:T(8,128)} %am_hbm.1), custom_call_target="tpu_custom_call" | custom-call | flops 6442450944 | bytes 4194304 | tf_op jit(solution)/shard_map/pallas_call | solution.py:286
  42.5 1.3 %shard_map.69 = (bf16[32,512]{1,0:T(8,128)(2,1)}, bf16[512,2048]{1,0:T(8,128)(2,1)}) custom-call(bf16[32,512]{1,0:T(8,128)(2,1)S(1)} %get-tuple-element.4.gh, bf16[512,2048]{1,0:T(8,128)(2,1)S(1)} %get-tuple-element.5.gw), custom_call_target="tpu_custom_call" | custom-call | tf_op jit(solution)/shard_map/pallas_call | solution.py:326
where the time goes:
time: 43.9 us; the launch traced here: 43.8 us
  Pallas kernels  43.2 us (98%)
  between operations  0.64 us (1%)
    pallas_call x1, Pallas kernels, per_device(): pl.pallas_call(functools.partial(kernel, ny, nx, nz), out_shape=(pltpu.VM...  41.8 us
    pallas_call x1, Pallas kernels, per_device(): pl.pallas_call(finish, out_shape=(jax.ShapeDtypeStruct((tb, feats), bf16)...  1.35 us

commit v1 on v0

--- a/solution.py
+++ b/solution.py
@@ -47,12 +47,12 @@
     other = lambda dy, dx: (lax.rem(y + dy, ny), lax.rem(x + dx, nx))
 
     barrier = pltpu.get_barrier_semaphore()
+    for k in far_z:
+        pl.semaphore_signal(barrier, inc=1, device_id={"dp": lax.rem(z + k, nz)}, device_id_type=MESH)
     for dy, dx in far_xy:
         oy, ox = other(dy, dx)
         pl.semaphore_signal(barrier, inc=1, device_id={"vocab": (oy * nx + ox) * 2 + core}, device_id_type=MESH)
     pl.semaphore_signal(barrier, inc=1, device_id={"vocab": twin}, device_id_type=MESH)
-    for k in far_z:
-        pl.semaphore_signal(barrier, inc=1, device_id={"dp": lax.rem(z + k, nz)}, device_id_type=MESH)
 
     local = [
         pltpu.make_async_copy(hid, rows.at[core, y, x], loc_sem.at[0]),

time: 43.9 us -> 43.3 us (0.986)
  Pallas kernels: 43.2 us -> 42.5 us
    pallas_call x1, Pallas kernels: 41.8 us -> 41.2 us  [per_device(): pl.pallas_call(functools.partial(kernel, ny, nx, nz), out_shape=(pltpu.VM...]
where the time goes in v1:
time: 43.3 us; the launch traced here: 43.2 us
  Pallas kernels  42.5 us (98%)
  between operations  0.64 us (1%)
    pallas_call x1, Pallas kernels, per_device(): pl.pallas_call(functools.partial(kernel, ny, nx, nz), out_shape=(pltpu.VM...  41.2 us
    pallas_call x1, Pallas kernels, per_device(): pl.pallas_call(finish, out_shape=(jax.ShapeDtypeStruct((tb, feats), bf16)...  1.35 us

profile of v1, /device:TPU:1, one launch (start us, length us, event | category | flops | bytes accessed | tf_op | source)
XLA Modules:
  0.0 43.2 jit_solution(16810188773203556684)
XLA Ops:
  0.6 41.2 %shard_map.68 = (bf16[32,512]{1,0:T(8,128)(2,1)S(1)}, bf16[512,2048]{1,0:T(8,128)(2,1)S(1)}) custom-call(s32[16]{0:T(128)} %len_hbm.1, bf16[32,512]{1,0:T(8,128)(2,1)} %hid.1, bf16[512,2048]{1,0:T(8,128)(2,1)} %w_hbm.1, f32[16,2048]{1,0:T(8,128)} %gp_hbm.1, s32[16,2048]{1,0:T(8,128)} %am_hbm.1), custom_call_target="tpu_custom_call" | custom-call | flops 6442450944 | bytes 4194304 | tf_op jit(solution)/shard_map/pallas_call | solution.py:286
  41.8 1.3 %shard_map.69 = (bf16[32,512]{1,0:T(8,128)(2,1)}, bf16[512,2048]{1,0:T(8,128)(2,1)}) custom-call(bf16[32,512]{1,0:T(8,128)(2,1)S(1)} %get-tuple-element.4.gh, bf16[512,2048]{1,0:T(8,128)(2,1)S(1)} %get-tuple-element.5.gw), custom_call_target="tpu_custom_call" | custom-call | tf_op jit(solution)/shard_map/pallas_call | solution.py:326
